TPU v7x, 32 devices: a whole 2x2x4 slice. The times are simulated.
32 devices in a mesh: blk: 8 (over y, x, core), rep: 4 (over z).
Axes of the slice: x: 2, y: 2, z: 4, core: 2. Of those that a mesh axis runs over, the one named last changes fastest.
Arguments:
- features: bfloat16 [4096, 512], P('blk'), may hold values from -2000 to 2000
- labels: int32 [4096], P('blk'), may hold values from 0 to 127
- w_first: bfloat16 [512, 512], replicated, may hold values from -0.25 to 0.25
- w_second: bfloat16 [512, 128], replicated, may hold values from -0.25 to 0.25
- block_rows: int32 [8, 4, 2, 2], P('blk', 'rep'), may hold values from 0 to 1, as said below
- block_cols: int32 [8, 4, 2, 2], P('blk', 'rep'), may hold values from 0 to 1
- block_vals: bfloat16 [8, 4, 2, 2, 256, 256], P('blk', 'rep')
Outputs:
- logits: bfloat16 [4096, 128], P('blk')
- grad_first: float32 [512, 512], replicated
- grad_second: float32 [512, 128], replicated
- loss: float32 [], replicated
Inputs may be any that keep to these rules, and one draw needn't show every extreme that they name: `block_rows`: slot (i, r, t, p) holds a block of shard i's rows against shard (i - r * 2 - t) mod 8's columns; the matrix A assembled from all slots is symmetric; slots whose values are all zero are padding.
All inputs are finite; a program needn't handle non-finite values.
Results may differ from a plain program's by a relative error of at most 0.0083.
Values may be sent and summed in bfloat16 or wider, within the bound.
A program may use at most 64 MiB of HBM per device.

v0:
```python
import math

import jax
import jax.numpy as jnp
from jax import lax
from jax.sharding import PartitionSpec as P

HOPS = 2


alpha_rate = 0.1


def passed_along(value, axis, by):
    size = lax.axis_size(axis)
    return lax.ppermute(value, axis, [(i, (i + by) % size) for i in range(size)])


def on_device(features, labels, w_first, w_second, block_rows, block_cols, block_vals):
    rows_all = features.shape[0]
    classes = w_second.shape[1]
    nrep = lax.axis_size("rep")
    rep_id = lax.axis_index("rep")
    share = rows_all // nrep
    nodes = rows_all * lax.axis_size("blk")
    index_rows = block_rows[0, 0]
    index_cols = block_cols[0, 0]
    tiles = block_vals[0, 0]
    steps = tiles.shape[0]
    slots = tiles.shape[1]
    width = tiles.shape[2]

    def add_step(total, step, panel):
        step_tiles = lax.dynamic_index_in_dim(tiles, step, 0, keepdims=False)
        step_rows = lax.dynamic_index_in_dim(index_rows, step, 0, keepdims=False)
        step_cols = lax.dynamic_index_in_dim(index_cols, step, 0, keepdims=False)
        for slot in range(slots):
            piece = lax.dynamic_slice_in_dim(panel, step_cols[slot] * width, width, 0)
            product = jnp.dot(step_tiles[slot], piece, preferred_element_type=jnp.float32)
            start = step_rows[slot] * width
            current = lax.dynamic_slice_in_dim(total, start, width, 0)
            total = lax.dynamic_update_slice_in_dim(total, current + product, start, 0)
        return total

    def propagate(panel):
        total = jnp.zeros((rows_all, classes), jnp.float32)
        near = panel
        for bit in range(nrep.bit_length() - 1):
            moved = passed_along(near, "blk", steps * (1 << bit))
            near = jnp.where(rep_id >> bit & 1 == 1, moved, near)

        def turn_one(turn, carry):
            acc, ahead = carry
            acc = add_step(acc, turn, ahead)
            ahead = passed_along(ahead, "blk", 1)
            return (acc, ahead)

        total, near = lax.fori_loop(0, steps - 1, turn_one, (total, near))
        total = add_step(total, steps - 1, near)
        return total

    def mine(full):
        return lax.dynamic_slice_in_dim(full, rep_id * share, share, 0)

    def reduce_rows(term):
        return lax.psum(term, "rep")

    def to_own(part_rows):
        return mine(part_rows)

    hidden = jax.nn.relu(jnp.dot(features, w_first, preferred_element_type=jnp.float32)).astype(
        jnp.bfloat16
    )
    base = jnp.dot(hidden, w_second, preferred_element_type=jnp.float32).astype(jnp.bfloat16)
    base_part = base.astype(jnp.float32)
    current = base
    for step in range(HOPS):
        mixed = (1.0 - alpha_rate) * reduce_rows(propagate(current)) + alpha_rate * base_part
        if step + 1 < HOPS:
            current = mixed.astype(jnp.bfloat16)
    logits = mixed.astype(jnp.bfloat16)
    onehot = (labels[:, None] == jnp.arange(classes, dtype=jnp.int32)[None, :]).astype(jnp.float32)
    lse = jax.nn.logsumexp(mixed, axis=1)
    picked = jnp.sum(mixed * onehot, axis=1)
    ce_sum = jnp.sum(to_own(lse - picked))
    grad_out = (jax.nn.softmax(mixed, axis=1) - onehot) * (1.0 / math.sqrt(nodes))
    grad_base = alpha_rate * grad_out
    moving = grad_out.astype(jnp.bfloat16)
    for step in range(HOPS):
        nxt = (1.0 - alpha_rate) * reduce_rows(propagate(moving))
        if step + 1 < HOPS:
            grad_base = grad_base + alpha_rate * nxt
            moving = nxt.astype(jnp.bfloat16)
        else:
            grad_base = grad_base + nxt
    grad_own = to_own(grad_base).astype(jnp.bfloat16)
    hidden_own = mine(hidden)
    feature_own = mine(features)
    grad_second = lax.dot_general(
        hidden_own, grad_own, (((0,), (0,)), ((), ())), preferred_element_type=jnp.float32
    )
    back = lax.dot_general(
        grad_own, w_second, (((1,), (1,)), ((), ())), preferred_element_type=jnp.float32
    )
    grad_hidden = jnp.where(hidden_own > 0, back, 0.0).astype(jnp.bfloat16)
    grad_first = lax.dot_general(
        feature_own, grad_hidden, (((0,), (0,)), ((), ())), preferred_element_type=jnp.float32
    )
    totals = lax.psum((grad_first, grad_second, ce_sum), ("blk", "rep"))
    return (logits, totals[0], totals[1], totals[2] / nodes)


def solution(mesh):
    in_specs = (
        P("blk", None),
        P("blk"),
        P(),
        P(),
        P("blk", "rep", None, None),
        P("blk", "rep", None, None),
        P("blk", "rep", None, None, None, None),
    )
    out_specs = (P("blk", None), P(), P(), P())
    return jax.shard_map(
        on_device, mesh=mesh, in_specs=in_specs, out_specs=out_specs, check_vma=False
    )
```

profile of v0, /device:TPU:1, one launch (start us, length us, event | category | flops | bytes accessed | tf_op | source)
XLA Modules:
  0.0 373.0 jit_solution(2840153545777894112)
XLA Ops:
  7.2 1.0 copy-done
  8.2 1.5 fusion
  10.0 2.1 collective-permute-start
  12.1 4.2 %collective-permute-done = bf16[512,128]{0,1:T(8,128)(2,1)S(1)} collective-permute-done((bf16[512,128]{0,1:T(8,128)(2,1)S(1)}, bf16[512,128]{0,1:T(8,128)(2,1)S(1)}, u32[]{:S(2)}, u32[]{:S(2)}) %collective-permute-start) | collective-permute-done | bytes 131104 | tf_op jit(solution)/shard_map/ppermute | solution.py:16
  16.3 1.2 collective-permute-start.1
  17.5 0.6 fusion.112
  20.7 0.6 fusion.111
  23.9 2.1 collective-permute-start.2
  26.4 1.5 collective-permute-done.2
  28.3 0.7 copy-done.3
  29.1 35.9 %all-reduce.7.cloned.1.call-done = f32[512,128]{0,1:T(8,128)} async-done(((f32[512,128]{0,1:T(8,128)}), f32[512,128]{0,1:T(8,128)}) %all-reduce.7.cloned.1.call-update) | async-done | bytes 262160 | tf_op jit(solution)/shard_map/psum | solution.py:66
  65.0 1.0 add_convert_fusion
  66.0 1.2 collective-permute-start.3
  67.2 3.5 collective-permute-done.3
  70.8 1.3 collective-permute-start.4
  72.0 2.6 collective-permute-done.4
  74.7 4.6 %collective-permute-start.5 = (bf16[512,128]{0,1:T(8,128)(2,1)S(1)}, bf16[512,128]{0,1:T(8,128)(2,1)S(1)}, u32[]{:S(2)}, u32[]{:S(2)}) collective-permute-start(bf16[512,128]{0,1:T(8,128)(2,1)S(1)} %broadcast_select_fusion.6), channel_id=1, source_target_pairs={{0,4},{4,8},{8,12},{12,16},{16,20},{20,24},{24,28},{28,0},{1,5},{5... | collective-permute-start | bytes 393224 | tf_op jit(solution)/shard_map/while/body/eval_jaxpr/ppermute | solution.py:16
  79.7 1.5 collective-permute-done.5
  81.6 0.7 copy-done.4
  82.4 35.4 %all-reduce.9.cloned.1.call-done = f32[512,128]{0,1:T(8,128)} async-done(((f32[512,128]{0,1:T(8,128)}), f32[512,128]{0,1:T(8,128)}) %all-reduce.9.cloned.1.call-update) | async-done | bytes 262160 | tf_op jit(solution)/shard_map/psum | solution.py:66
  117.8 1.0 fusion.110
  118.9 0.7 copy-done.9
  119.7 1.2 collective-permute-start.6
  121.0 3.5 collective-permute-done.6
  124.5 1.3 collective-permute-start.7
  125.8 2.6 collective-permute-done.7
  128.4 4.6 %collective-permute-start.8 = (bf16[512,128]{0,1:T(8,128)(2,1)S(1)}, bf16[512,128]{0,1:T(8,128)(2,1)S(1)}, u32[]{:S(2)}, u32[]{:S(2)}) collective-permute-start(bf16[512,128]{0,1:T(8,128)(2,1)S(1)} %broadcast_select_fusion.5), channel_id=1, source_target_pairs={{0,4},{4,8},{8,12},{12,16},{16,20},{20,24},{24,28},{28,0},{1,5},{5... | collective-permute-start | bytes 393224 | tf_op jit(solution)/shard_map/while/body/eval_jaxpr/ppermute | solution.py:16
  133.4 1.5 collective-permute-done.8
  135.4 0.7 copy-done.5
  136.1 35.5 %all-reduce.11.cloned.1.call-done = f32[512,128]{0,1:T(8,128)} async-done(((f32[512,128]{0,1:T(8,128)}), f32[512,128]{0,1:T(8,128)}) %all-reduce.11.cloned.1.call-update) | async-done | bytes 262160 | tf_op jit(solution)/shard_map/psum | solution.py:66
  171.6 1.0 multiply_convert_fusion
  172.6 1.2 collective-permute-start.9
  173.9 3.5 collective-permute-done.9
  177.5 1.3 collective-permute-start.10
  178.7 2.6 collective-permute-done.10
  181.4 4.6 %collective-permute-start.11 = (bf16[512,128]{0,1:T(8,128)(2,1)S(1)}, bf16[512,128]{0,1:T(8,128)(2,1)S(1)}, u32[]{:S(2)}, u32[]{:S(2)}) collective-permute-start(bf16[512,128]{0,1:T(8,128)(2,1)S(1)} %broadcast_select_fusion.4), channel_id=1, source_target_pairs={{0,4},{4,8},{8,12},{12,16},{16,20},{20,24},{24,28},{28,0},{1,5},{5... | collective-permute-start | bytes 393224 | tf_op jit(solution)/shard_map/while/body/eval_jaxpr/ppermute | solution.py:16
  186.4 1.5 collective-permute-done.11
  188.3 0.7 copy-done.2
  189.1 35.4 %all-reduce.13.cloned.1.call-done = f32[512,128]{0,1:T(8,128)} async-done(((f32[512,128]{0,1:T(8,128)}), f32[512,128]{0,1:T(8,128)}) %all-reduce.13.cloned.1.call-update) | async-done | bytes 262160 | tf_op jit(solution)/shard_map/psum | solution.py:66
  224.5 0.9 fusion.71
  225.3 0.9 fusion.51
  226.3 1.4 fusion.2
  227.8 0.7 dynamic-slice_reduce_fusion
  228.4 41.6 %psum.55 = f32[]{:T(128)} all-reduce(f32[]{:T(128)} %dynamic-slice_reduce_fusion), channel_id=1, replica_groups=mesh['blk'=8,'rep'=4] {'blk','rep'}, use_global_device_ids=true, to_apply=%region_11.12 | all-reduce | flops 1 | bytes 8 | tf_op jit(solution)/shard_map/psum | solution.py:109
  270.1 0.8 copy.11
  271.5 90.9 %all-reduce.15.cloned.1.call-done = (f32[512,512]{1,0:T(8,128)}, f32[512,128]{1,0:T(8,128)}) async-done(((f32[512,512]{1,0:T(8,128)}, f32[512,128]{1,0:T(8,128)}), (f32[512,512]{1,0:T(8,128)}, f32[512,128]{1,0:T(8,128)})) %all-reduce.15.cloned.1.call-update) | async-done | bytes 1310736 | tf_op jit(solution)/shard_map/psum | solution.py:109
  362.3 2.3 copy.34
  364.6 0.7 copy.35
  (62 shorter events, 4.2 us)
Async XLA Ops:
  7.2 1.0 copy-start
  7.2 2.5 copy-start.7
  7.2 57.8 %all-reduce.7.cloned.1.call-start = ((), (), s32[]{:S(2)}) async-start(), calls=%async_computation | async-start | bytes 524288 | tf_op jit(solution)/shard_map/psum | solution.py:66
  9.7 7.8 %copy-start.10 = (s32[1,1,2,2]{3,2,1,0:T(2,128)S(1)}, s32[1,1,2,2]{3,2,1,0:T(2,128)}, u32[]{:S(2)}) copy-start(s32[1,1,2,2]{3,2,1,0:T(2,128)} %param.11) | copy-start | bytes 52
  9.7 11.0 %copy-start.11 = (s32[1,1,2,2]{3,2,1,0:T(2,128)S(1)}, s32[1,1,2,2]{3,2,1,0:T(2,128)}, u32[]{:S(2)}) copy-start(s32[1,1,2,2]{3,2,1,0:T(2,128)} %param.12) | copy-start | bytes 52
  10.0 6.3 %collective-permute-start = (bf16[512,128]{0,1:T(8,128)(2,1)S(1)}, bf16[512,128]{0,1:T(8,128)(2,1)S(1)}, u32[]{:S(2)}, u32[]{:S(2)}) collective-permute-start(bf16[512,128]{0,1:T(8,128)(2,1)S(1)} %convolution_convert_fusion), channel_id=1, source_target_pairs={{0,8},{4,12},{8,16},{12,20},{16,24},{20,28},{24,0},{28,4},{1,9},{5... | collective-permute-start | bytes 393224 | tf_op jit(solution)/shard_map/ppermute | solution.py:16
  12.1 13.9 %copy-start.1 = (bf16[1,1,2,2,256,256]{5,4,3,2,1,0:T(8,128)(2,1)S(1)}, bf16[1,1,2,2,256,256]{5,4,3,2,1,0:T(8,128)(2,1)}, u32[]{:S(2)}) copy-start(bf16[1,1,2,2,256,256]{5,4,3,2,1,0:T(8,128)(2,1)} %param.13) | copy-start | bytes 1572868
  16.3 7.5 %collective-permute-start.1 = (bf16[512,128]{0,1:T(8,128)(2,1)S(1)}, bf16[512,128]{0,1:T(8,128)(2,1)S(1)}, u32[]{:S(2)}, u32[]{:S(2)}) collective-permute-start(bf16[512,128]{0,1:T(8,128)(2,1)S(1)} %broadcast_select_fusion.3), channel_id=1, source_target_pairs={{0,16},{4,20},{8,24},{12,28},{16,0},{20,4},{24,8},{28,12},{1,17},{... | collective-permute-start | bytes 393224 | tf_op jit(solution)/shard_map/ppermute | solution.py:16
  23.9 4.0 %collective-permute-start.2 = (bf16[512,128]{0,1:T(8,128)(2,1)S(1)}, bf16[512,128]{0,1:T(8,128)(2,1)S(1)}, u32[]{:S(2)}, u32[]{:S(2)}) collective-permute-start(bf16[512,128]{0,1:T(8,128)(2,1)S(1)} %broadcast_select_fusion.7), channel_id=1, source_target_pairs={{0,4},{4,8},{8,12},{12,16},{16,20},{20,24},{24,28},{28,0},{1,5},{5... | collective-permute-start | bytes 393224 | tf_op jit(solution)/shard_map/while/body/eval_jaxpr/ppermute | solution.py:16
  28.3 0.7 copy-start.3
  29.1 88.8 %all-reduce.9.cloned.1.call-start = ((), (), s32[]{:S(2)}) async-start(), calls=%async_computation.1 | async-start | bytes 524288 | tf_op jit(solution)/shard_map/psum | solution.py:66
  66.0 4.8 %collective-permute-start.3 = (bf16[512,128]{0,1:T(8,128)(2,1)S(1)}, bf16[512,128]{0,1:T(8,128)(2,1)S(1)}, u32[]{:S(2)}, u32[]{:S(2)}) collective-permute-start(bf16[512,128]{0,1:T(8,128)(2,1)S(1)} %add_convert_fusion), channel_id=1, source_target_pairs={{0,8},{4,12},{8,16},{12,20},{16,24},{20,28},{24,0},{28,4},{1,9},{5... | collective-permute-start | bytes 393224 | tf_op jit(solution)/shard_map/ppermute | solution.py:16
  70.8 3.9 %collective-permute-start.4 = (bf16[512,128]{0,1:T(8,128)(2,1)S(1)}, bf16[512,128]{0,1:T(8,128)(2,1)S(1)}, u32[]{:S(2)}, u32[]{:S(2)}) collective-permute-start(bf16[512,128]{0,1:T(8,128)(2,1)S(1)} %broadcast_select_fusion.2), channel_id=1, source_target_pairs={{0,16},{4,20},{8,24},{12,28},{16,0},{20,4},{24,8},{28,12},{1,17},{... | collective-permute-start | bytes 393224 | tf_op jit(solution)/shard_map/ppermute | solution.py:16
  74.7 6.5 %collective-permute-start.5 = (bf16[512,128]{0,1:T(8,128)(2,1)S(1)}, bf16[512,128]{0,1:T(8,128)(2,1)S(1)}, u32[]{:S(2)}, u32[]{:S(2)}) collective-permute-start(bf16[512,128]{0,1:T(8,128)(2,1)S(1)} %broadcast_select_fusion.6), channel_id=1, source_target_pairs={{0,4},{4,8},{8,12},{12,16},{16,20},{20,24},{24,28},{28,0},{1,5},{5... | collective-permute-start | bytes 393224 | tf_op jit(solution)/shard_map/while/body/eval_jaxpr/ppermute | solution.py:16
  81.6 0.7 copy-start.4
  82.4 89.2 %all-reduce.11.cloned.1.call-start = ((), (), s32[]{:S(2)}) async-start(), calls=%async_computation.2 | async-start | bytes 524288 | tf_op jit(solution)/shard_map/psum | solution.py:66
  118.8 0.7 copy-start.9
  119.7 4.8 %collective-permute-start.6 = (bf16[512,128]{0,1:T(8,128)(2,1)S(1)}, bf16[512,128]{0,1:T(8,128)(2,1)S(1)}, u32[]{:S(2)}, u32[]{:S(2)}) collective-permute-start(bf16[512,128]{0,1:T(8,128)(2,1)S(1)} %get-tuple-element.76), channel_id=1, source_target_pairs={{0,8},{4,12},{8,16},{12,20},{16,24},{20,28},{24,0},{28,4},{1,9},{5... | collective-permute-start | bytes 393224 | tf_op jit(solution)/shard_map/ppermute | solution.py:16
  124.5 3.9 %collective-permute-start.7 = (bf16[512,128]{0,1:T(8,128)(2,1)S(1)}, bf16[512,128]{0,1:T(8,128)(2,1)S(1)}, u32[]{:S(2)}, u32[]{:S(2)}) collective-permute-start(bf16[512,128]{0,1:T(8,128)(2,1)S(1)} %broadcast_select_fusion.1), channel_id=1, source_target_pairs={{0,16},{4,20},{8,24},{12,28},{16,0},{20,4},{24,8},{28,12},{1,17},{... | collective-permute-start | bytes 393224 | tf_op jit(solution)/shard_map/ppermute | solution.py:16
  128.4 6.5 %collective-permute-start.8 = (bf16[512,128]{0,1:T(8,128)(2,1)S(1)}, bf16[512,128]{0,1:T(8,128)(2,1)S(1)}, u32[]{:S(2)}, u32[]{:S(2)}) collective-permute-start(bf16[512,128]{0,1:T(8,128)(2,1)S(1)} %broadcast_select_fusion.5), channel_id=1, source_target_pairs={{0,4},{4,8},{8,12},{12,16},{16,20},{20,24},{24,28},{28,0},{1,5},{5... | collective-permute-start | bytes 393224 | tf_op jit(solution)/shard_map/while/body/eval_jaxpr/ppermute | solution.py:16
  135.4 0.7 copy-start.5
  136.1 88.4 %all-reduce.13.cloned.1.call-start = ((), (), s32[]{:S(2)}) async-start(), calls=%async_computation.3 | async-start | bytes 524288 | tf_op jit(solution)/shard_map/psum | solution.py:66
  171.6 5.8 %copy-start.6 = (f32[512,128]{0,1:T(8,128)S(1)}, f32[512,128]{0,1:T(8,128)}, u32[]{:S(2)}) copy-start(f32[512,128]{0,1:T(8,128)} %all-reduce.11.cloned.1.call-done) | copy-start | bytes 786436
  172.6 4.8 %collective-permute-start.9 = (bf16[512,128]{0,1:T(8,128)(2,1)S(1)}, bf16[512,128]{0,1:T(8,128)(2,1)S(1)}, u32[]{:S(2)}, u32[]{:S(2)}) collective-permute-start(bf16[512,128]{0,1:T(8,128)(2,1)S(1)} %multiply_convert_fusion), channel_id=1, source_target_pairs={{0,8},{4,12},{8,16},{12,20},{16,24},{20,28},{24,0},{28,4},{1,9},{5... | collective-permute-start | bytes 393224 | tf_op jit(solution)/shard_map/ppermute | solution.py:16
  177.5 3.9 %collective-permute-start.10 = (bf16[512,128]{0,1:T(8,128)(2,1)S(1)}, bf16[512,128]{0,1:T(8,128)(2,1)S(1)}, u32[]{:S(2)}, u32[]{:S(2)}) collective-permute-start(bf16[512,128]{0,1:T(8,128)(2,1)S(1)} %broadcast_select_fusion), channel_id=1, source_target_pairs={{0,16},{4,20},{8,24},{12,28},{16,0},{20,4},{24,8},{28,12},{1,17},{... | collective-permute-start | bytes 393224 | tf_op jit(solution)/shard_map/ppermute | solution.py:16
  181.4 6.5 %collective-permute-start.11 = (bf16[512,128]{0,1:T(8,128)(2,1)S(1)}, bf16[512,128]{0,1:T(8,128)(2,1)S(1)}, u32[]{:S(2)}, u32[]{:S(2)}) collective-permute-start(bf16[512,128]{0,1:T(8,128)(2,1)S(1)} %broadcast_select_fusion.4), channel_id=1, source_target_pairs={{0,4},{4,8},{8,12},{12,16},{16,20},{20,24},{24,28},{28,0},{1,5},{5... | collective-permute-start | bytes 393224 | tf_op jit(solution)/shard_map/while/body/eval_jaxpr/ppermute | solution.py:16
  188.3 0.7 copy-start.2
  189.0 173.3 %all-reduce.15.cloned.1.call-start = ((), (), s32[]{:S(2)}) async-start(), calls=%async_computation.4 | async-start | bytes 2621440 | tf_op jit(solution)/shard_map/psum | solution.py:109
  362.3 2.3 copy-start.8
Sparse Core Ops, SparseCore 0:
  29.2 35.7 all-reduce.6
  82.5 35.2 all-reduce.8
  136.2 35.3 all-reduce.10
  189.1 35.2 all-reduce.12
  230.3 131.9 all-reduce.14
where the time goes:
time: 375 us; the launch traced here: 373 us
  waiting for transfers between devices  262 us (70%)
  blocking collectives  41.6 us (11%)
  starting transfers between devices  26.8 us (7%)
  between operations  21 us (6%)
  local copies, waits for them, and re-layouts  9.49 us (3%)
  matrix products  7.31 us (2%)
  other arithmetic  4.96 us (1%)
    psum x4, waiting for transfers between devices, reduce_rows(): return lax.psum(term, 'rep')  142 us
    psum x1, waiting for transfers between devices, on_device(): totals = lax.psum((grad_first, grad_second, ce_sum), ('blk', 'rep'))  90.9 us
    psum x1, blocking collectives, on_device(): totals = lax.psum((grad_first, grad_second, ce_sum), ('blk', 'rep'))  41.6 us
    ppermute x12, waiting for transfers between devices, passed_along(): lax.ppermute(value, axis, [(i, (i + by) % size) for i in range(size)])  28.7 us
    ppermute x12, starting transfers between devices, passed_along(): lax.ppermute(value, axis, [(i, (i + by) % size) for i in range(size)])  26.6 us
    unnamed x27, local copies, waits for them, and re-layouts  8.24 us
  transfers between devices with their start and end apart: 17, of which 16 were waited for; matrix products, arithmetic and copies ran while one was open for 1% of the time, Pallas kernels for 0%

commit v1 on v0

v1 whole, which is shorter than its diff:
```python
import functools
import math

import jax
import jax.numpy as jnp
from jax import lax
from jax.experimental import pallas as pl
from jax.experimental.pallas import tpu as pltpu
from jax.sharding import PartitionSpec as P

HOPS = 2
MESH = pl.DeviceIdType.MESH
F32 = jnp.float32
BF16 = jnp.bfloat16

alpha_rate = 0.1


def dot(a, b, dims=((1,), (0,))):
    return lax.dot_general(a, b, (dims, ((), ())), preferred_element_type=F32)


def graph_kernel(nblk, nrep, finish, *refs):
    feat, lab, w1, w2, brow, bcol, bval = refs[:7]
    if finish:
        logits_o, sums_o, ce_o = refs[7:10]
        refs = refs[10:]
    else:
        logits_o, hidden_o, gb_o, ce_o = refs[7:11]
        refs = refs[11:]
    (hidden, base, onehot, acc, scat_send, scat_recv, panel, piece, red_send, red_recv,
     logit_buf, gb_buf, ce_rep, ce_blk, grads, grads_recv, sums,
     scat_ss, scat_rs, mc_ss, mc_rs, red_ss, red_rs, lg_ss, lg_rs, gb_ss, gb_rs,
     cr_ss, cr_rs, cb_ss, cb_rs, gr_ss, gr_rs, az_ss, az_rs, al_ss, al_rs, ac_ss, ac_rs) = refs
    i = lax.axis_index("blk")
    q = lax.axis_index("rep")
    rows, classes = base.shape
    steps, slots, width = bval.shape[2], bval.shape[3], bval.shape[4]
    share = rows // nrep
    nrb = rows // width
    pending = []

    def copy(src, dst, ss, rs, blk, rep):
        return pltpu.make_async_remote_copy(
            src_ref=src, dst_ref=dst, send_sem=ss, recv_sem=rs,
            device_id=(blk, rep), device_id_type=MESH)

    def send(src, dst, ss, rs, blk, rep):
        one = copy(src, dst, ss, rs, blk, rep)
        one.start()
        pending.append(one)

    def arrived(dst, ss, rs):
        copy(dst, dst, ss, rs, i, q).wait_recv()

    def part_of(r):
        return pl.ds(pl.multiple_of(r * share, share), share)

    def beside(x):
        return jnp.concatenate([x[n * width:(n + 1) * width] for n in range(nrb)], axis=1)

    def placed(totals, prod, out_block, in_block):
        at = jnp.full((width, classes), out_block * nrb + in_block, jnp.int32)
        for n in range(nrb):
            for m in range(nrb):
                term = prod[:, m * classes:(m + 1) * classes]
                totals[n] = totals[n] + jnp.where(at == n * nrb + m, term, 0.0)
        return totals

    mine = part_of(q)

    barrier = pltpu.get_barrier_semaphore()
    everyone = nblk * nrep

    def greet(n, carry):
        pl.semaphore_signal(
            barrier, inc=1,
            device_id=(lax.rem(i + n // nrep, nblk), lax.rem(q + n % nrep, nrep)),
            device_id_type=MESH)
        return carry

    if everyone <= 64:
        for n in range(1, everyone):
            greet(n, 0)
    else:
        lax.fori_loop(1, everyone, greet, 0)

    hidden[...] = jnp.maximum(dot(feat[...], w1[...]), 0.0).astype(BF16)
    base[...] = dot(hidden[...], w2[...]).astype(BF16)
    for t in range(steps):
        totals = [jnp.zeros((width, classes), F32) for _ in range(nrb)]
        wide = beside(base[...])
        for p in range(slots):
            prod = dot(bval[0, 0, t, p], wide, ((0,), (0,)))
            totals = placed(totals, prod, bcol[0, 0, t, p], brow[0, 0, t, p])
        for n in range(nrb):
            scat_send[t, n * width:(n + 1) * width, :] = totals[n].astype(BF16)

    pl.semaphore_wait(barrier, everyone - 1)

    for d in list(range(1, nrep)) + [0]:
        r = lax.rem(q + d, nrep)
        for t in range(steps):
            to = lax.rem(i + 2 * nblk - q * steps - t, nblk)
            src = scat_send.at[t, part_of(r)]
            dst = scat_recv.at[t, d]
            if d == 0 and t == 0:
                own = copy(src, dst, scat_ss.at[t, d], scat_rs.at[t, d], to, r)
                pl.when(q != 0)(own.start)

                @pl.when(q == 0)
                def _():
                    scat_recv[0, 0] = scat_send[0, part_of(r)]
            else:
                send(src, dst, scat_ss.at[t, d], scat_rs.at[t, d], to, r)
    scat_own = own

    classes_down = lax.broadcasted_iota(jnp.int32, (classes, rows), 0)
    onehot[...] = jnp.where(lab[...] == classes_down, 1.0, 0.0).astype(F32).T

    total = jnp.zeros((share, classes), F32)
    for d in range(nrep):
        for t in range(steps):
            dst = scat_recv.at[t, d]
            if d == 0 and t == 0:
                @pl.when(q != 0)
                def _():
                    arrived(scat_recv.at[0, 0], scat_ss.at[0, 0], scat_rs.at[0, 0])
            else:
                arrived(dst, scat_ss.at[t, d], scat_rs.at[t, d])
            total = total + scat_recv[t, d].astype(F32)
    base_part = alpha_rate * base[mine, :].astype(F32)
    mc_own = []

    def spread(k, value):
        piece[k] = value
        for d in list(range(1, nrep)) + [0]:
            r = lax.rem(q + d, nrep)
            for t in range(steps):
                to = lax.rem(i + r * steps + t, nblk)
                dst = panel.at[k, t, mine]
                if d == 0 and t == 0:
                    own = copy(piece.at[k], dst, mc_ss.at[k, t, d], mc_rs.at[k, t, d], to, r)
                    pl.when(q != 0)(own.start)
                    mc_own.append(own)

                    @pl.when(q == 0)
                    def _():
                        panel[k, 0, mine, :] = value
                else:
                    send(piece.at[k], dst, mc_ss.at[k, t, d], mc_rs.at[k, t, d], to, r)

    def multiply(k):
        totals = [jnp.zeros((width, classes), F32) for _ in range(nrb)]
        for t in range(steps):
            for d in range(nrep):
                dst = panel.at[k, t, part_of(lax.rem(q + nrep - d, nrep))]
                if d == 0 and t == 0:
                    @pl.when(q != 0)
                    def _():
                        arrived(dst, mc_ss.at[k, 0, 0], mc_rs.at[k, 0, 0])
                else:
                    arrived(dst, mc_ss.at[k, t, d], mc_rs.at[k, t, d])
            wide = beside(panel[k, t])
            for p in range(slots):
                prod = dot(bval[0, 0, t, p], wide)
                totals = placed(totals, prod, brow[0, 0, t, p], bcol[0, 0, t, p])
        for n in range(nrb):
            acc[n * width:(n + 1) * width, :] = totals[n]
            red_send[k, n * width:(n + 1) * width, :] = totals[n].astype(BF16)
        for d in range(1, nrep):
            r = lax.rem(q + d, nrep)
            send(red_send.at[k, part_of(r)], red_recv.at[k, d],
                 red_ss.at[k, d], red_rs.at[k, d], i, r)
        out = acc[mine, :]
        for d in range(1, nrep):
            arrived(red_recv.at[k, d], red_ss.at[k, d], red_rs.at[k, d])
            out = out + red_recv[k, d].astype(F32)
        return out

    def to_reps(buf, ss, rs):
        for d in range(1, nrep):
            send(buf.at[mine], buf.at[mine], ss.at[d], rs.at[d], i, lax.rem(q + d, nrep))

    def from_reps(buf, ss, rs):
        for d in range(1, nrep):
            arrived(buf.at[part_of(lax.rem(q + nrep - d, nrep))], ss.at[d], rs.at[d])

    spread(0, ((1.0 - alpha_rate) * total + base_part).astype(BF16))
    mixed = (1.0 - alpha_rate) * multiply(0) + base_part
    hot = onehot[mine, :]
    top = jnp.max(mixed, axis=1, keepdims=True)
    exps = jnp.exp(mixed - top)
    norm = jnp.sum(exps, axis=1, keepdims=True)
    grad_out = (exps / norm - hot) * (1.0 / math.sqrt(rows * nblk))
    spread(1, grad_out.astype(BF16))
    logit_buf[mine, :] = mixed.astype(BF16)
    to_reps(logit_buf, lg_ss, lg_rs)
    ce = top + jnp.log(norm) - jnp.sum(mixed * hot, axis=1, keepdims=True)
    ce_rep[0] = jnp.broadcast_to(jnp.sum(ce, axis=0, keepdims=True), ce_rep.shape[1:])
    if finish:
        for d in range(1, nrep):
            send(ce_rep.at[0], ce_rep.at[d], cr_ss.at[d], cr_rs.at[d], i, lax.rem(q + d, nrep))

    step_one = (1.0 - alpha_rate) * multiply(1)
    spread(2, step_one.astype(BF16))
    grad_base = alpha_rate * grad_out + alpha_rate * step_one
    grad_base = grad_base + (1.0 - alpha_rate) * multiply(2)
    grad_b = grad_base.astype(BF16)

    if finish:
        gb_buf[mine, :] = grad_b
        to_reps(gb_buf, gb_ss, gb_rs)
        part = hidden.shape[1] // nrep
        cols = pl.ds(pl.multiple_of(q * part, part), part)
        hid = hidden[:, cols]
        second = w2[cols, :]
        loss = ce_rep[0]
        for d in range(1, nrep):
            arrived(ce_rep.at[d], cr_ss.at[d], cr_rs.at[d])
            loss = loss + ce_rep[d]
        ce_blk[0] = loss
        from_reps(gb_buf, gb_ss, gb_rs)
        gb = gb_buf[...]
        back = dot(gb, second, ((1,), (1,)))
        gh = jnp.where(hid > 0, back, 0.0).astype(BF16)
        fcount = feat.shape[1]
        grads[:fcount, :] = dot(feat[...], gh, ((0,), (0,))).astype(BF16)
        grads[fcount:, :] = dot(hid, gb, ((0,), (0,))).astype(BF16)
        chunk = grads.shape[0] // nblk

        def chunk_of(b):
            return pl.ds(pl.multiple_of(b * chunk, chunk), chunk)

        for e in range(1, nblk):
            to = lax.rem(i + e, nblk)
            send(grads.at[chunk_of(to)], grads_recv.at[e], gr_ss.at[e], gr_rs.at[e], to, q)
        for e in range(1, nblk):
            to = lax.rem(i + e, nblk)
            send(ce_blk.at[0], ce_blk.at[e], cb_ss.at[e], cb_rs.at[e], to, q)
        whole = grads[chunk_of(i), :].astype(F32)
        for e in range(1, nblk):
            arrived(grads_recv.at[e], gr_ss.at[e], gr_rs.at[e])
            whole = whole + grads_recv[e].astype(F32)
        sums[q, chunk_of(i), :] = whole.astype(BF16)
        here = sums.at[q, chunk_of(i)]
        for d in range(1, nrep):
            send(here, here, az_ss.at[d], az_rs.at[d], i, lax.rem(q + d, nrep))
        half = nblk // 2
        partner = i + 1 - 2 * lax.rem(i, 2)
        for d in range(nrep):
            block = sums.at[lax.rem(q + nrep - d, nrep), chunk_of(i)]
            if d:
                arrived(block, az_ss.at[d], az_rs.at[d])
            for e in range(1, half):
                send(block, block, al_ss.at[d, e], al_rs.at[d, e], lax.rem(i + 2 * e, nblk), q)
            send(block, block, ac_ss.at[d, 0], ac_rs.at[d, 0], partner, q)
        for d in range(nrep):
            for e in range(1, half):
                block = sums.at[lax.rem(q + nrep - d, nrep),
                                chunk_of(lax.rem(i + nblk - 2 * e, nblk))]
                arrived(block, al_ss.at[d, e], al_rs.at[d, e])
                send(block, block, ac_ss.at[d, e], ac_rs.at[d, e], partner, q)
        for e in range(1, nblk):
            arrived(ce_blk.at[e], cb_ss.at[e], cb_rs.at[e])
            loss = loss + ce_blk[e]
        ce_o[...] = loss
        from_reps(logit_buf, lg_ss, lg_rs)
        logits_o[...] = logit_buf[...]
        for d in range(nrep):
            for e in range(half):
                block = sums.at[lax.rem(q + nrep - d, nrep),
                                chunk_of(lax.rem(partner + nblk - 2 * e, nblk))]
                arrived(block, ac_ss.at[d, e], ac_rs.at[d, e])
        sums_o[...] = sums[...]
    else:
        gb_o[...] = grad_b
        hidden_o[...] = hidden[...]
        ce_o[...] = ce_rep[0]
        from_reps(logit_buf, lg_ss, lg_rs)
        logits_o[...] = logit_buf[...]

    for one in pending:
        one.wait_send()
    for one in [scat_own] + mc_own:
        pl.when(q != 0)(one.wait_send)


def on_device(features, labels, w_first, w_second, block_rows, block_cols, block_vals):
    rows, fcount = features.shape
    hcount, classes = w_second.shape
    nblk = lax.axis_size("blk")
    nrep = lax.axis_size("rep")
    steps = block_vals.shape[2]
    share = rows // nrep
    nodes = rows * nblk
    tall = fcount + hcount // nrep
    finish = (nblk % 2 == 0 and hcount // nrep == classes and tall % (16 * nblk) == 0)
    chunk = tall // nblk if finish else 16
    tall = tall if finish else 16
    sdma = pltpu.SemaphoreType.DMA
    vmem = pl.BlockSpec(memory_space=pltpu.VMEM)
    smem = pl.BlockSpec(memory_space=pltpu.SMEM)
    if finish:
        outs = [((rows, classes), BF16), ((nrep, tall, classes), BF16), ((8, 128), F32)]
    else:
        outs = [((rows, classes), BF16), ((rows, hcount), BF16), ((share, classes), BF16),
                ((8, 128), F32)]
    back = HOPS + 1
    scratch = [
        pltpu.VMEM((rows, hcount), BF16),
        pltpu.VMEM((rows, classes), BF16),
        pltpu.VMEM((rows, classes), F32),
        pltpu.VMEM((rows, classes), F32),
        pltpu.VMEM((steps, rows, classes), BF16),
        pltpu.VMEM((steps, nrep, share, classes), BF16),
        pltpu.VMEM((back, steps, rows, classes), BF16),
        pltpu.VMEM((back, share, classes), BF16),
        pltpu.VMEM((back, rows, classes), BF16),
        pltpu.VMEM((back, nrep, share, classes), BF16),
        pltpu.VMEM((rows, classes), BF16),
        pltpu.VMEM((rows, classes), BF16),
        pltpu.VMEM((nrep, 8, 128), F32),
        pltpu.VMEM((nblk, 8, 128), F32),
        pltpu.VMEM((tall, classes), BF16),
        pltpu.VMEM((nblk, chunk, classes), BF16),
        pltpu.VMEM((nrep, tall, classes), BF16),
    ]
    for shape in ((steps, nrep), (back, steps, nrep), (back, nrep), (nrep,), (nrep,), (nrep,),
                  (nblk,), (nblk,), (nrep,), (nrep, nblk // 2), (nrep, nblk // 2)):
        scratch += [sdma(shape), sdma(shape)]
    results = pl.pallas_call(
        functools.partial(graph_kernel, nblk, nrep, finish),
        out_shape=[jax.ShapeDtypeStruct(*one) for one in outs],
        in_specs=[vmem, vmem, vmem, vmem, smem, smem, vmem],
        out_specs=[vmem] * len(outs),
        scratch_shapes=scratch,
        compiler_params=pltpu.CompilerParams(
            collective_id=0, has_side_effects=True, vmem_limit_bytes=40 * 1024 * 1024),
    )(features, labels.reshape(1, rows), w_first, w_second, block_rows, block_cols, block_vals)
    if finish:
        logits, sums, ce = results
        grad_first = jnp.swapaxes(sums[:, :fcount], 0, 1).reshape(fcount, hcount).astype(F32)
        grad_second = sums[:, fcount:].reshape(hcount, classes).astype(F32)
        return (logits, grad_first, grad_second, ce[0, 0] / nodes)

    logits, hidden, grad_own, ce = results
    rep_id = lax.axis_index("rep")

    def own(full):
        return lax.dynamic_slice_in_dim(full, rep_id * share, share, 0)

    hidden_own = own(hidden)
    grad_second = dot(hidden_own, grad_own, ((0,), (0,)))
    grad_hidden = jnp.where(hidden_own > 0, dot(grad_own, w_second, ((1,), (1,))), 0.0)
    grad_first = dot(own(features), grad_hidden.astype(BF16), ((0,), (0,)))
    totals = lax.psum((grad_first, grad_second, ce[0, 0]), ("blk", "rep"))
    return (logits, totals[0], totals[1], totals[2] / nodes)


def solution(mesh):
    in_specs = (
        P("blk", None),
        P("blk"),
        P(),
        P(),
        P("blk", "rep", None, None),
        P("blk", "rep", None, None),
        P("blk", "rep", None, None, None, None),
    )
    out_specs = (P("blk", None), P(), P(), P())
    return jax.shard_map(
        on_device, mesh=mesh, in_specs=in_specs, out_specs=out_specs, check_vma=False
    )
```

time: 375 us -> 85.6 us (0.23)
  waiting for transfers between devices: 262 us -> 0 us
  Pallas kernels: 0 us -> 73.1 us
  blocking collectives: 41.6 us -> 0 us
  starting transfers between devices: 26.8 us -> 0 us
  between operations: 21 us -> 2.46 us
  matrix products: 7.31 us -> 0 us
  other arithmetic: 4.96 us -> 0.8 us
    psum x5 -> x0, waiting for transfers between devices: 233 us -> none  [the longest x4 142 us: reduce_rows(): return lax.psum(term, 'rep')]
    pallas_call x0 -> x1, Pallas kernels: none -> 73.1 us  [on_device(): pl.pallas_call(functools.partial(graph_kernel, nblk, nrep, finish), out_s...]
    psum x1 -> x0, blocking collectives: 41.6 us -> none  [on_device(): totals = lax.psum((grad_first, grad_second, ce_sum), ('blk', 'rep'))]
    ppermute x12 -> x0, waiting for transfers between devices: 28.7 us -> none  [passed_along(): lax.ppermute(value, axis, [(i, (i + by) % size) for i in range(size)])]
    ppermute x12 -> x0, starting transfers between devices: 26.6 us -> none  [passed_along(): lax.ppermute(value, axis, [(i, (i + by) % size) for i in range(size)])]
    dot_general x20 -> x0, matrix products: 7.31 us -> none  [the longest x16 3.16 us: add_step(): jnp.dot(step_tiles[slot], piece, preferred_element_type=jnp.float32)]
    unnamed x27 -> x16, local copies, waits for them, and re-layouts: 8.24 us -> 8.02 us
  transfers between devices with their start and end apart: 17 -> 0, of which waited for: 16 -> 0; matrix products, arithmetic and copies ran while one was open for 1% -> 0% of each run, Pallas kernels for 0% -> 0%
where the time goes in v1:
time: 85.6 us; the launch traced here: 85.2 us
  Pallas kernels  73.1 us (85%)
  local copies, waits for them, and re-layouts  8.88 us (10%)
  between operations  2.46 us (3%)
    pallas_call x1, Pallas kernels, on_device(): pl.pallas_call(functools.partial(graph_kernel, nblk, nrep, finish), out_s...  73.1 us
    unnamed x16, local copies, waits for them, and re-layouts  8.02 us

profile of v1, /device:TPU:1, one launch (start us, length us, event | category | flops | bytes accessed | tf_op | source)
XLA Modules:
  0.0 85.2 jit_solution(8243522765850978344)
XLA Ops:
  0.6 0.0 copy-start.5
  0.6 0.7 copy-done.5
  1.3 0.0 copy-start
  1.3 1.0 %copy-done = bf16[512,512]{1,0:T(8,128)(2,1)S(1)} copy-done((bf16[512,512]{1,0:T(8,128)(2,1)S(1)}, bf16[512,512]{1,0:T(8,128)(2,1)}, u32[]{:S(2)}) %copy-start) | copy-done | bytes 524312
  2.4 0.0 copy-start.1
  2.4 1.0 %copy-done.1 = bf16[512,512]{1,0:T(8,128)(2,1)S(1)} copy-done((bf16[512,512]{1,0:T(8,128)(2,1)S(1)}, bf16[512,512]{1,0:T(8,128)(2,1)}, u32[]{:S(2)}) %copy-start.1) | copy-done | bytes 524312
  3.4 0.0 copy-start.2
  3.4 1.0 %copy-done.2 = bf16[1,1,2,2,256,256]{5,4,3,2,1,0:T(8,128)(2,1)S(1)} copy-done((bf16[1,1,2,2,256,256]{5,4,3,2,1,0:T(8,128)(2,1)S(1)}, bf16[1,1,2,2,256,256]{5,4,3,2,1,0:T(8,128)(2,1)}, u32[]{:S(2)}) %copy-start.2) | copy-done | bytes 524312
  4.4 0.0 copy-start.3
  4.4 0.9 %copy-done.3 = bf16[512,128]{1,0:T(8,128)(2,1)S(1)} copy-done((bf16[512,128]{1,0:T(8,128)(2,1)S(1)}, bf16[512,128]{1,0:T(8,128)(2,1)}, u32[]{:S(2)}) %copy-start.3) | copy-done | bytes 131096
  5.3 0.0 copy-start.4
  5.3 0.7 copy-done.4
  6.0 0.0 copy-start.6
  6.0 0.7 copy-done.6
  6.7 73.1 %shard_map.102 = (bf16[512,128]{1,0:T(8,128)(2,1)S(1)}, bf16[4,640,128]{2,1,0:T(8,128)(2,1)S(1)}, f32[8,128]{1,0:T(8,128)S(1)}) custom-call(bf16[512,512]{1,0:T(8,128)(2,1)S(1)} %copy-done, s32[1,512]{1,0:T(1,128)S(1)} %bitcast.8, bf16[512,512]{1,0:T(8,128)(2,1)S(1)} %copy-done.1, bf16[512,128]{1,0:T(8,128)(2,1)S(1)} %copy-done.3, ...), custom_call_target="tpu_custom_call" | custom-call | tf_op jit(solution)/shard_map/pallas_call | solution.py:332
  79.8 0.5 slice.11
  81.0 0.7 bitcast_convert_fusion
  81.7 0.1 convert_bitcast_fusion
  81.8 0.3 copy.11
  82.1 1.3 %copy.12 = f32[512,512]{1,0:T(8,128)} copy(f32[512,512]{0,1:T(8,128)S(1)} %bitcast.9) | data formatting | bytes 2097152
  83.4 0.7 copy.14
  (1 shorter events, 0.0 us)
Async XLA Ops:
  0.6 0.7 copy-start.5
  1.3 1.0 %copy-start = (bf16[512,512]{1,0:T(8,128)(2,1)S(1)}, bf16[512,512]{1,0:T(8,128)(2,1)}, u32[]{:S(2)}) copy-start(bf16[512,512]{1,0:T(8,128)(2,1)} %refs_0_.1) | copy-start | bytes 1572868
  2.4 1.0 %copy-start.1 = (bf16[512,512]{1,0:T(8,128)(2,1)S(1)}, bf16[512,512]{1,0:T(8,128)(2,1)}, u32[]{:S(2)}) copy-start(bf16[512,512]{1,0:T(8,128)(2,1)} %refs_2_.1) | copy-start | bytes 1572868
  3.4 1.0 %copy-start.2 = (bf16[1,1,2,2,256,256]{5,4,3,2,1,0:T(8,128)(2,1)S(1)}, bf16[1,1,2,2,256,256]{5,4,3,2,1,0:T(8,128)(2,1)}, u32[]{:S(2)}) copy-start(bf16[1,1,2,2,256,256]{5,4,3,2,1,0:T(8,128)(2,1)} %refs_6_.1) | copy-start | bytes 1572868
  4.4 0.9 %copy-start.3 = (bf16[512,128]{1,0:T(8,128)(2,1)S(1)}, bf16[512,128]{1,0:T(8,128)(2,1)}, u32[]{:S(2)}) copy-start(bf16[512,128]{1,0:T(8,128)(2,1)} %refs_3_.1) | copy-start | bytes 393220
  5.3 0.7 copy-start.4
  6.0 0.7 copy-start.6

commit v2 on v1

--- a/solution.py
+++ b/solution.py
@@ -21,13 +21,20 @@
 
 
 def graph_kernel(nblk, nrep, finish, *refs):
-    feat, lab, w1, w2, brow, bcol, bval = refs[:7]
-    if finish:
-        logits_o, sums_o, ce_o = refs[7:10]
-        refs = refs[10:]
+    given = refs[:7]
+    if finish:
+        logits_o, first_o, second_o, ce_o = refs[7:11]
+        refs = refs[11:]
     else:
         logits_o, hidden_o, gb_o, ce_o = refs[7:11]
         refs = refs[11:]
+    feat, lab, w1, w2, brow, bcol, bval = refs[:7]
+    load_sem, feat_t, hid_t, second_t = refs[7:11]
+    loads = [pltpu.make_async_copy(src, dst, load_sem.at[n])
+             for n, (src, dst) in enumerate(zip(given, refs[:7]))]
+    for n in (0, 2, 3, 6, 4, 5, 1):
+        loads[n].start()
+    refs = refs[11:]
     (hidden, base, onehot, acc, scat_send, scat_recv, panel, piece, red_send, red_recv,
      logit_buf, gb_buf, ce_rep, ce_blk, grads, grads_recv, sums,
      scat_ss, scat_rs, mc_ss, mc_rs, red_ss, red_rs, lg_ss, lg_rs, gb_ss, gb_rs,
@@ -59,8 +66,11 @@
     def beside(x):
         return jnp.concatenate([x[n * width:(n + 1) * width] for n in range(nrb)], axis=1)
 
+    def spot(ref, t, p):
+        return ref[0, 0, t:t + 1, p:p + 1]
+
     def placed(totals, prod, out_block, in_block):
-        at = jnp.full((width, classes), out_block * nrb + in_block, jnp.int32)
+        at = jnp.broadcast_to(out_block * nrb + in_block, (width, classes))
         for n in range(nrb):
             for m in range(nrb):
                 term = prod[:, m * classes:(m + 1) * classes]
@@ -85,14 +95,19 @@
     else:
         lax.fori_loop(1, everyone, greet, 0)
 
+    loads[0].wait()
+    loads[2].wait()
     hidden[...] = jnp.maximum(dot(feat[...], w1[...]), 0.0).astype(BF16)
+    loads[3].wait()
     base[...] = dot(hidden[...], w2[...]).astype(BF16)
+    for n in (4, 5, 6):
+        loads[n].wait()
     for t in range(steps):
         totals = [jnp.zeros((width, classes), F32) for _ in range(nrb)]
         wide = beside(base[...])
         for p in range(slots):
             prod = dot(bval[0, 0, t, p], wide, ((0,), (0,)))
-            totals = placed(totals, prod, bcol[0, 0, t, p], brow[0, 0, t, p])
+            totals = placed(totals, prod, spot(bcol, t, p), spot(brow, t, p))
         for n in range(nrb):
             scat_send[t, n * width:(n + 1) * width, :] = totals[n].astype(BF16)
 
@@ -115,6 +130,7 @@
                 send(src, dst, scat_ss.at[t, d], scat_rs.at[t, d], to, r)
     scat_own = own
 
+    loads[1].wait()
     classes_down = lax.broadcasted_iota(jnp.int32, (classes, rows), 0)
     onehot[...] = jnp.where(lab[...] == classes_down, 1.0, 0.0).astype(F32).T
 
@@ -164,7 +180,7 @@
             wide = beside(panel[k, t])
             for p in range(slots):
                 prod = dot(bval[0, 0, t, p], wide)
-                totals = placed(totals, prod, brow[0, 0, t, p], bcol[0, 0, t, p])
+                totals = placed(totals, prod, spot(brow, t, p), spot(bcol, t, p))
         for n in range(nrb):
             acc[n * width:(n + 1) * width, :] = totals[n]
             red_send[k, n * width:(n + 1) * width, :] = totals[n].astype(BF16)
@@ -186,7 +202,16 @@
         for d in range(1, nrep):
             arrived(buf.at[part_of(lax.rem(q + nrep - d, nrep))], ss.at[d], rs.at[d])
 
+    def ahead():
+        part = hidden.shape[1] // nrep
+        cols = pl.ds(pl.multiple_of(q * part, part), part)
+        feat_t[...] = feat[...].T
+        hid_t[...] = hidden[:, cols].T
+        second_t[...] = w2[cols, :].T
+
     spread(0, ((1.0 - alpha_rate) * total + base_part).astype(BF16))
+    if finish:
+        ahead()
     mixed = (1.0 - alpha_rate) * multiply(0) + base_part
     hot = onehot[mine, :]
     top = jnp.max(mixed, axis=1, keepdims=True)
@@ -195,7 +220,6 @@
     grad_out = (exps / norm - hot) * (1.0 / math.sqrt(rows * nblk))
     spread(1, grad_out.astype(BF16))
     logit_buf[mine, :] = mixed.astype(BF16)
-    to_reps(logit_buf, lg_ss, lg_rs)
     ce = top + jnp.log(norm) - jnp.sum(mixed * hot, axis=1, keepdims=True)
     ce_rep[0] = jnp.broadcast_to(jnp.sum(ce, axis=0, keepdims=True), ce_rep.shape[1:])
     if finish:
@@ -214,19 +238,19 @@
         part = hidden.shape[1] // nrep
         cols = pl.ds(pl.multiple_of(q * part, part), part)
         hid = hidden[:, cols]
-        second = w2[cols, :]
         loss = ce_rep[0]
         for d in range(1, nrep):
             arrived(ce_rep.at[d], cr_ss.at[d], cr_rs.at[d])
             loss = loss + ce_rep[d]
         ce_blk[0] = loss
         from_reps(gb_buf, gb_ss, gb_rs)
+        to_reps(logit_buf, lg_ss, lg_rs)
         gb = gb_buf[...]
-        back = dot(gb, second, ((1,), (1,)))
+        back = dot(gb, second_t[...])
         gh = jnp.where(hid > 0, back, 0.0).astype(BF16)
         fcount = feat.shape[1]
-        grads[:fcount, :] = dot(feat[...], gh, ((0,), (0,))).astype(BF16)
-        grads[fcount:, :] = dot(hid, gb, ((0,), (0,))).astype(BF16)
+        grads[:fcount, :] = dot(feat_t[...], gh).astype(BF16)
+        grads[fcount:, :] = dot(hid_t[...], gb).astype(BF16)
         chunk = grads.shape[0] // nblk
 
         def chunk_of(b):
@@ -272,8 +296,11 @@
                 block = sums.at[lax.rem(q + nrep - d, nrep),
                                 chunk_of(lax.rem(partner + nblk - 2 * e, nblk))]
                 arrived(block, ac_ss.at[d, e], ac_rs.at[d, e])
-        sums_o[...] = sums[...]
+        for r in range(nrep):
+            first_o[:, r * part:(r + 1) * part] = sums[r, :fcount]
+            second_o[r * part:(r + 1) * part, :] = sums[r, fcount:]
     else:
+        to_reps(logit_buf, lg_ss, lg_rs)
         gb_o[...] = grad_b
         hidden_o[...] = hidden[...]
         ce_o[...] = ce_rep[0]
@@ -300,14 +327,22 @@
     tall = tall if finish else 16
     sdma = pltpu.SemaphoreType.DMA
     vmem = pl.BlockSpec(memory_space=pltpu.VMEM)
-    smem = pl.BlockSpec(memory_space=pltpu.SMEM)
-    if finish:
-        outs = [((rows, classes), BF16), ((nrep, tall, classes), BF16), ((8, 128), F32)]
+    hbm = pl.BlockSpec(memory_space=pltpu.HBM)
+    if finish:
+        outs = [((rows, classes), BF16), ((fcount, hcount), BF16), ((hcount, classes), BF16),
+                ((8, 128), F32)]
     else:
         outs = [((rows, classes), BF16), ((rows, hcount), BF16), ((share, classes), BF16),
                 ((8, 128), F32)]
     back = HOPS + 1
-    scratch = [
+    operands = (features, labels.reshape(1, rows), w_first, w_second,
+                block_rows, block_cols, block_vals)
+    part = hcount // nrep
+    scratch = [pltpu.VMEM(one.shape, one.dtype) for one in operands] + [
+        sdma((len(operands),)),
+        pltpu.VMEM((fcount, rows), BF16),
+        pltpu.VMEM((part, rows), BF16),
+        pltpu.VMEM((classes, part), BF16),
         pltpu.VMEM((rows, hcount), BF16),
         pltpu.VMEM((rows, classes), BF16),
         pltpu.VMEM((rows, classes), F32),
@@ -332,17 +367,15 @@
     results = pl.pallas_call(
         functools.partial(graph_kernel, nblk, nrep, finish),
         out_shape=[jax.ShapeDtypeStruct(*one) for one in outs],
-        in_specs=[vmem, vmem, vmem, vmem, smem, smem, vmem],
+        in_specs=[hbm] * len(operands),
         out_specs=[vmem] * len(outs),
         scratch_shapes=scratch,
         compiler_params=pltpu.CompilerParams(
-            collective_id=0, has_side_effects=True, vmem_limit_bytes=40 * 1024 * 1024),
-    )(features, labels.reshape(1, rows), w_first, w_second, block_rows, block_cols, block_vals)
-    if finish:
-        logits, sums, ce = results
-        grad_first = jnp.swapaxes(sums[:, :fcount], 0, 1).reshape(fcount, hcount).astype(F32)
-        grad_second = sums[:, fcount:].reshape(hcount, classes).astype(F32)
-        return (logits, grad_first, grad_second, ce[0, 0] / nodes)
+            collective_id=0, has_side_effects=True, vmem_limit_bytes=64 * 1024 * 1024 - 65536),
+    )(*operands)
+    if finish:
+        logits, first, second, ce = results
+        return (logits, first.astype(F32), second.astype(F32), ce[0, 0] / nodes)
 
     logits, hidden, grad_own, ce = results
     rep_id = lax.axis_index("rep")

time: 85.6 us -> 79.4 us (0.928)
  local copies, waits for them, and re-layouts: 8.88 us -> 1.85 us
  other arithmetic: 0.8 us -> 2.9 us
  Pallas kernels: 73.1 us -> 72 us
    unnamed x16 -> x5, local copies, waits for them, and re-layouts: 8.02 us -> 0.67 us
    convert_element_type x2, other arithmetic: 0.8 us -> 2.9 us  [on_device(): return (logits, first.astype(F32), second.astype(F32), ce[0, 0] / nodes)]
    pallas_call x1, Pallas kernels: 73.1 us -> 72 us  [on_device(): pl.pallas_call(functools.partial(graph_kernel, nblk, nrep, finish), out_s...]
where the time goes in v2:
time: 79.4 us; the launch traced here: 79.2 us
  Pallas kernels  72 us (91%)
  other arithmetic  2.9 us (4%)
  between operations  2.44 us (3%)
  local copies, waits for them, and re-layouts  1.85 us (2%)
    pallas_call x1, Pallas kernels, on_device(): pl.pallas_call(functools.partial(graph_kernel, nblk, nrep, finish), out_s...  72 us
    convert_element_type x2, other arithmetic, on_device(): return (logits, first.astype(F32), second.astype(F32), ce[0, 0] / nodes)  2.9 us

profile of v2, /device:TPU:1, one launch (start us, length us, event | category | flops | bytes accessed | tf_op | source)
XLA Modules:
  0.0 79.2 jit_solution(4915137232147428837)
XLA Ops:
  0.6 72.0 %shard_map.102 = (bf16[512,128]{1,0:T(8,128)(2,1)}, bf16[512,512]{1,0:T(8,128)(2,1)}, bf16[512,128]{1,0:T(8,128)(2,1)}, f32[8,128]{1,0:T(8,128)}) custom-call(bf16[512,512]{1,0:T(8,128)(2,1)} %refs_0_.1, s32[1,512]{1,0:T(1,128)} %bitcast.2, bf16[512,512]{1,0:T(8,128)(2,1)} %refs_2_.1, bf16[512,128]{1,0:T(8,128)(2,1)} %refs_3_.1, s32[1,1,2,2]{3,2,1,0:T(2,128)} %refs_4_.1, ...), custom_call_target="tpu_custom_call" | custom-call | tf_op jit(solution)/shard_map/pallas_call | solution.py:367
  72.7 0.0 copy-start
  72.7 2.2 %convert_element_type.6 = f32[512,512]{1,0:T(8,128)} convert(bf16[512,512]{1,0:T(8,128)(2,1)} %get-tuple-element.9) | non-fusion elementwise | flops 262144 | bytes 1572864 | tf_op jit(solution)/shard_map/convert_element_type | solution.py:378
  74.9 0.0 copy-done
  74.9 0.0 copy-start.1
  74.9 0.7 convert_element_type.7
  75.6 1.2 %slice.3 = f32[1,1]{1,0:T(1,128)} slice(f32[8,128]{1,0:T(8,128)} %get-tuple-element.11), slice={[0:1], [0:1]} | slice | bytes 8 | tf_op jit(solution)/shard_map/slice | solution.py:378
  77.4 0.0 copy-done.1
  77.4 0.7 copy.12
Async XLA Ops:
  72.7 2.2 %copy-start = (bf16[512,128]{1,0:T(8,128)(2,1)S(1)}, bf16[512,128]{1,0:T(8,128)(2,1)}, u32[]{:S(2)}) copy-start(bf16[512,128]{1,0:T(8,128)(2,1)} %get-tuple-element.10) | copy-start | bytes 393220
  74.9 2.6 %copy-start.1 = (bf16[512,128]{1,0:T(8,128)(2,1)S(1)}, bf16[512,128]{1,0:T(8,128)(2,1)}, u32[]{:S(2)}) copy-start(bf16[512,128]{1,0:T(8,128)(2,1)} %get-tuple-element.16) | copy-start | bytes 393220

commit v3 on v2

--- a/solution.py
+++ b/solution.py
@@ -152,19 +152,18 @@
         piece[k] = value
         for d in list(range(1, nrep)) + [0]:
             r = lax.rem(q + d, nrep)
-            for t in range(steps):
-                to = lax.rem(i + r * steps + t, nblk)
-                dst = panel.at[k, t, mine]
-                if d == 0 and t == 0:
-                    own = copy(piece.at[k], dst, mc_ss.at[k, t, d], mc_rs.at[k, t, d], to, r)
-                    pl.when(q != 0)(own.start)
-                    mc_own.append(own)
-
-                    @pl.when(q == 0)
-                    def _():
-                        panel[k, 0, mine, :] = value
-                else:
-                    send(piece.at[k], dst, mc_ss.at[k, t, d], mc_rs.at[k, t, d], to, r)
+            to = lax.rem(i + r * steps, nblk)
+            dst = panel.at[k, 0, mine]
+            if d == 0:
+                own = copy(piece.at[k], dst, mc_ss.at[k, 0, 0], mc_rs.at[k, 0, 0], to, r)
+                pl.when(q != 0)(own.start)
+                mc_own.append(own)
+
+                @pl.when(q == 0)
+                def _():
+                    panel[k, 0, mine, :] = value
+            else:
+                send(piece.at[k], dst, mc_ss.at[k, 0, d], mc_rs.at[k, 0, d], to, r)
 
     def multiply(k):
         totals = [jnp.zeros((width, classes), F32) for _ in range(nrb)]
@@ -177,6 +176,10 @@
                         arrived(dst, mc_ss.at[k, 0, 0], mc_rs.at[k, 0, 0])
                 else:
                     arrived(dst, mc_ss.at[k, t, d], mc_rs.at[k, t, d])
+                if t + 1 < steps:
+                    rows_of = part_of(lax.rem(q + nrep - d, nrep))
+                    send(dst, panel.at[k, t + 1, rows_of], mc_ss.at[k, t + 1, d],
+                         mc_rs.at[k, t + 1, d], lax.rem(i + 1, nblk), q)
             wide = beside(panel[k, t])
             for p in range(slots):
                 prod = dot(bval[0, 0, t, p], wide)
@@ -288,7 +291,7 @@
         for e in range(1, nblk):
             arrived(ce_blk.at[e], cb_ss.at[e], cb_rs.at[e])
             loss = loss + ce_blk[e]
-        ce_o[...] = loss
+        ce_o[...] = loss[:1, :1] * (1.0 / (rows * nblk))
         from_reps(logit_buf, lg_ss, lg_rs)
         logits_o[...] = logit_buf[...]
         for d in range(nrep):
@@ -297,8 +300,8 @@
                                 chunk_of(lax.rem(partner + nblk - 2 * e, nblk))]
                 arrived(block, ac_ss.at[d, e], ac_rs.at[d, e])
         for r in range(nrep):
-            first_o[:, r * part:(r + 1) * part] = sums[r, :fcount]
-            second_o[r * part:(r + 1) * part, :] = sums[r, fcount:]
+            first_o[:, r * part:(r + 1) * part] = sums[r, :fcount].astype(F32)
+            second_o[r * part:(r + 1) * part, :] = sums[r, fcount:].astype(F32)
     else:
         to_reps(logit_buf, lg_ss, lg_rs)
         gb_o[...] = grad_b
@@ -329,8 +332,8 @@
     vmem = pl.BlockSpec(memory_space=pltpu.VMEM)
     hbm = pl.BlockSpec(memory_space=pltpu.HBM)
     if finish:
-        outs = [((rows, classes), BF16), ((fcount, hcount), BF16), ((hcount, classes), BF16),
-                ((8, 128), F32)]
+        outs = [((rows, classes), BF16), ((fcount, hcount), F32), ((hcount, classes), F32),
+                ((1, 1), F32)]
     else:
         outs = [((rows, classes), BF16), ((rows, hcount), BF16), ((share, classes), BF16),
                 ((8, 128), F32)]
@@ -375,7 +378,7 @@
     )(*operands)
     if finish:
         logits, first, second, ce = results
-        return (logits, first.astype(F32), second.astype(F32), ce[0, 0] / nodes)
+        return (logits, first, second, ce.reshape(()))
 
     logits, hidden, grad_own, ce = results
     rep_id = lax.axis_index("rep")

time: 79.4 us -> 77.8 us (0.980)
  other arithmetic: 2.9 us -> 0 us
  local copies, waits for them, and re-layouts: 1.85 us -> 4.58 us
  Pallas kernels: 72 us -> 70.7 us
    unnamed x5, local copies, waits for them, and re-layouts: 0.67 us -> 4.58 us
    convert_element_type x2 -> x0, other arithmetic: 2.9 us -> none  [on_device(): return (logits, first.astype(F32), second.astype(F32), ce[0, 0] / nodes)]
    pallas_call x1, Pallas kernels: 72 us -> 70.7 us  [on_device(): pl.pallas_call(functools.partial(graph_kernel, nblk, nrep, finish), out_s...]
    slice x1 -> x0, local copies, waits for them, and re-layouts: 1.18 us -> none  [on_device(): return (logits, first.astype(F32), second.astype(F32), ce[0, 0] / nodes)]
where the time goes in v3:
time: 77.8 us; the launch traced here: 77.6 us
  Pallas kernels  70.7 us (91%)
  local copies, waits for them, and re-layouts  4.58 us (6%)
  between operations  2.39 us (3%)
    pallas_call x1, Pallas kernels, on_device(): pl.pallas_call(functools.partial(graph_kernel, nblk, nrep, finish), out_s...  70.7 us
    unnamed x5, local copies, waits for them, and re-layouts  4.58 us

profile of v3, /device:TPU:1, one launch (start us, length us, event | category | flops | bytes accessed | tf_op | source)
XLA Modules:
  0.0 77.6 jit_solution(8127653196646452515)
XLA Ops:
  0.6 70.7 %shard_map.102 = (bf16[512,128]{1,0:T(8,128)(2,1)}, f32[512,512]{1,0:T(8,128)}, f32[512,128]{1,0:T(8,128)}, f32[1,1]{1,0:T(1,128)}) custom-call(bf16[512,512]{1,0:T(8,128)(2,1)} %refs_0_.1, s32[1,512]{1,0:T(1,128)} %bitcast.2, bf16[512,512]{1,0:T(8,128)(2,1)} %refs_2_.1, bf16[512,128]{1,0:T(8,128)(2,1)} %refs_3_.1, s32[1,1,2,2]{3,2,1,0:T(2,128)} %refs_4_.1, ...), custom_call_target="tpu_custom_call" | custom-call | tf_op jit(solution)/shard_map/pallas_call | solution.py:370
  71.3 1.6 %copy.15 = bf16[512,128]{1,0:T(8,128)(2,1)} copy(bf16[512,128]{1,0:T(8,128)(2,1)} %get-tuple-element.16) | data formatting | bytes 262144
  72.9 0.0 copy-start
  72.9 2.3 %copy.16 = f32[512,512]{1,0:T(8,128)} copy(f32[512,512]{1,0:T(8,128)} %get-tuple-element.17) | data formatting | bytes 2097152
  75.2 0.0 copy-done
  75.2 0.7 copy.17
Async XLA Ops:
  72.9 2.3 %copy-start = (f32[512,128]{1,0:T(8,128)S(1)}, f32[512,128]{1,0:T(8,128)}, u32[]{:S(2)}) copy-start(f32[512,128]{1,0:T(8,128)} %get-tuple-element.18) | copy-start | bytes 786436
